TPU v7x, 128 devices: a whole 4x4x4 slice. The times are simulated.
128 devices in a mesh: seq: 64 (over x_lo, y, z, core), mp: 2 (over x_hi).
Axes of the slice: x: 4 (x_hi: 2, x_lo: 2; x = x_hi * 2 + x_lo), y: 4, z: 4, core: 2. Of those that a mesh axis runs over, the one named last changes fastest.
Arguments:
- tokens: bfloat16 [16384, 2048], P('seq'), may hold values from -16 to 16
- cotangent: bfloat16 [16384, 2048], P('seq'), may hold values from -16 to 16
- next_kv_grad: bfloat16 [16384, 256], P('seq'), may hold values from -6 to 6
- seq_lengths: int32 [6], replicated, may hold values from 1024 to 4096, as said below
- pad_counts: int32 [6], replicated, may hold values from 0 to 1024, as said below
- norm_attn: float32 [2048], replicated, may hold values from 0.1 to 1.9
- norm_ffn: float32 [2048], replicated, may hold values from 0.1 to 1.9
- w_query: bfloat16 [2048, 2048], P(None, 'mp'), may hold values from -0.125 to 0.125
- w_keyval: bfloat16 [2048, 256], replicated, may hold values from -0.125 to 0.125
- w_out: bfloat16 [2048, 2048], P('mp'), may hold values from -0.5 to 0.5
- w_gate: bfloat16 [2048, 5632], P(None, 'mp'), may hold values from -0.125 to 0.125
- w_up: bfloat16 [2048, 5632], P(None, 'mp'), may hold values from -0.125 to 0.125
- w_down: bfloat16 [5632, 2048], P('mp'), may hold values from -0.078125 to 0.078125
Outputs:
- mixed: bfloat16 [16384, 2048], P('seq')
- input_grad: bfloat16 [16384, 2048], P('seq')
- shared_kv: bfloat16 [16384, 256], P('seq')
- shared_grad: float32 [16384, 256], P('seq')
- grad_norm_attn: float32 [2048], P('seq')
- grad_norm_ffn: float32 [2048], P('seq')
- grad_query: float32 [2048, 2048], P('seq', 'mp')
- grad_keyval: float32 [2048, 256], P('seq')
- grad_out: float32 [2048, 2048], P('mp', 'seq')
- grad_gate: float32 [2048, 5632], P('seq', 'mp')
- grad_up: float32 [2048, 5632], P('seq', 'mp')
- grad_down: float32 [5632, 2048], P('mp', 'seq')
Inputs may be any that keep to these rules, and one draw needn't show every extreme that they name: `seq_lengths`: 6 lengths in token order, summing to 16384, each at least min(1024, 4096); one is exactly 4096. `pad_counts`: at most a quarter of the sequence's length, rounded down; a sequence of length 4096 has exactly 1024.
All inputs are finite; a program needn't handle non-finite values.
Results may differ from a plain program's by a relative error of at most 0.017.
Values may be sent and summed in bfloat16 or wider, within the bound.
No kernel may reach another device: no remote copies, remote signals or barrier semaphores. Data moves between devices by JAX's collectives and lax.ppermute only.
A program may use at most 320 MiB of HBM per device.

v0:
```python
import jax
import jax.numpy as jnp
from jax import lax
from jax.sharding import PartitionSpec as P

HD = 128
WINDOW = 512


EPSILON = 1e-05
THETA = 10000.0
MASKED = -1e30


def shifted(value, axis, steps):
    count = lax.axis_size(axis)
    initial, last = (max(0, -steps), min(count, count - steps))
    return lax.ppermute(value, axis, [(source, source + steps) for source in range(initial, last)])


def rounded(value):
    return lax.optimization_barrier(value.astype(jnp.bfloat16)).astype(jnp.float32)


def contract_rows(left, right):
    return lax.dot_general(
        left, right, (((0,), (0,)), ((), ())), preferred_element_type=jnp.float32
    )


def contract_cols(left, right):
    return lax.dot_general(
        left, right, (((1,), (1,)), ((), ())), preferred_element_type=jnp.float32
    )


def token_facts(token_idx, seq_lengths, pad_counts):
    ends = jnp.cumsum(seq_lengths)
    which = jnp.sum((token_idx[:, None] >= ends[None, :]).astype(jnp.int32), axis=1)
    member = which[:, None] == jnp.arange(seq_lengths.shape[0], dtype=jnp.int32)[None, :]
    begin = jnp.sum(jnp.where(member, (ends - seq_lengths)[None, :], 0), axis=1)
    live = jnp.sum(jnp.where(member, (seq_lengths - pad_counts)[None, :], 0), axis=1)
    place = token_idx - begin
    return (jnp.where(token_idx >= 0, which, -1), place, place < live)


def rotation(place):
    half = HD // 2
    freqs = jnp.exp(-jnp.log(THETA) * jnp.arange(half, dtype=jnp.float32) * 2.0 / HD)
    angle = place.astype(jnp.float32)[:, None] * freqs[None, :]
    return (jnp.cos(angle), jnp.sin(angle))


def rotate(value, cos_table, sin_table):
    half = value.shape[-1] // 2
    lower_half = value[..., :half]
    upper_half = value[..., half:]
    return jnp.concatenate(
        [
            lower_half * cos_table - upper_half * sin_table,
            upper_half * cos_table + lower_half * sin_table,
        ],
        axis=-1,
    )


def unrotate(value, cos_table, sin_table):
    half = value.shape[-1] // 2
    lower_half = value[..., :half]
    upper_half = value[..., half:]
    return jnp.concatenate(
        [
            lower_half * cos_table + upper_half * sin_table,
            upper_half * cos_table - lower_half * sin_table,
        ],
        axis=-1,
    )


def norm_back(d_normed, normed, inverse):
    return inverse * (d_normed - normed * jnp.mean(d_normed * normed, axis=-1, keepdims=True))


def shards(
    tokens,
    cotangent,
    next_kv_grad,
    seq_lengths,
    pad_counts,
    norm_attn,
    norm_ffn,
    w_query,
    w_keyval,
    w_out,
    w_gate,
    w_up,
    w_down,
):
    tok_rows = tokens.shape[0]
    rim_shards = (WINDOW + tok_rows - 1) // tok_rows
    rim_rows = rim_shards * tok_rows
    first_row = lax.axis_index("seq") * tok_rows
    own_idx = first_row + jnp.arange(tok_rows, dtype=jnp.int32)
    key_idx = first_row - rim_rows + jnp.arange(rim_rows + tok_rows, dtype=jnp.int32)
    seq_q, place_q, real_q = token_facts(own_idx, seq_lengths, pad_counts)
    seq_k, place_k, real_k = token_facts(key_idx, seq_lengths, pad_counts)
    allowed = (
        (seq_q[:, None] == seq_k[None, :])
        & (key_idx[None, :] <= own_idx[:, None])
        & (own_idx[:, None] - key_idx[None, :] < WINDOW)
        & (real_k[None, :] | (key_idx[None, :] == own_idx[:, None]))
    )
    cos_table, sin_table = rotation(place_q)
    head_cnt = w_query.shape[1] // HD
    scale = HD ** (-0.5)
    x_full = tokens.astype(jnp.float32)
    inv_a = lax.rsqrt(jnp.mean(x_full * x_full, axis=-1, keepdims=True) + EPSILON)
    normed_a = x_full * inv_a
    hid_a = (normed_a * norm_attn).astype(jnp.bfloat16)
    query = jnp.dot(hid_a, w_query, preferred_element_type=jnp.float32).reshape(
        tok_rows, head_cnt, HD
    )
    query = rotate(query, cos_table[:, None, :], sin_table[:, None, :]).astype(jnp.bfloat16)
    keyval = jnp.dot(hid_a, w_keyval, preferred_element_type=jnp.float32)
    shared = jnp.concatenate(
        [rotate(keyval[:, :HD], cos_table, sin_table), keyval[:, HD:]], axis=1
    ).astype(jnp.bfloat16)
    rim_pieces = [shifted(shared, "seq", offset) for offset in range(rim_shards, 0, -1)]
    keys_all = jnp.concatenate(rim_pieces + [shared], axis=0)

    def scores_of(key_rows):
        scores = (
            jnp.einsum("qhd,kd->hqk", query, key_rows[:, :HD], preferred_element_type=jnp.float32)
            * scale
        )
        return jnp.where(allowed[None], scores, MASKED)

    scores = scores_of(keys_all)
    row_max = jnp.max(scores, axis=-1, keepdims=True)
    exps = jnp.exp(scores - row_max)
    row_total = jnp.sum(exps, axis=-1, keepdims=True)
    prob = (exps / row_total).astype(jnp.bfloat16)
    log_total = row_max + jnp.log(row_total)
    attn = jnp.einsum("hqk,kd->qhd", prob, keys_all[:, HD:], preferred_element_type=jnp.float32)
    attn = attn.reshape(tok_rows, head_cnt * HD).astype(jnp.bfloat16)
    branch_attn = lax.psum(
        jnp.dot(attn, w_out, preferred_element_type=jnp.float32).astype(jnp.bfloat16), "mp"
    ).astype(jnp.float32)
    middle = x_full + branch_attn
    inv_b = lax.rsqrt(jnp.mean(middle * middle, axis=-1, keepdims=True) + EPSILON)
    normed_b = middle * inv_b
    hid_b = (normed_b * norm_ffn).astype(jnp.bfloat16)
    gate = jnp.dot(hid_b, w_gate, preferred_element_type=jnp.float32)
    upval = jnp.dot(hid_b, w_up, preferred_element_type=jnp.float32)
    sigm = jax.nn.sigmoid(gate)
    act = (gate * sigm * upval).astype(jnp.bfloat16)
    branch_ffn = lax.psum(
        jnp.dot(act, w_down, preferred_element_type=jnp.float32).astype(jnp.bfloat16), "mp"
    ).astype(jnp.float32)
    mixed = (middle + branch_ffn).astype(jnp.bfloat16)
    d_out = cotangent.astype(jnp.float32)
    g_down = contract_rows(act, cotangent)
    d_act = rounded(contract_cols(cotangent, w_down))
    d_gate = (d_act * upval * sigm * (1.0 + gate * (1.0 - sigm))).astype(jnp.bfloat16)
    d_up = (d_act * gate * sigm).astype(jnp.bfloat16)
    g_gate = contract_rows(hid_b, d_gate)
    g_up = contract_rows(hid_b, d_up)
    d_hid_b = lax.psum(
        (contract_cols(d_gate, w_gate) + contract_cols(d_up, w_up)).astype(jnp.bfloat16), "mp"
    ).astype(jnp.float32)
    g_gain_b = jnp.sum(d_hid_b * normed_b, axis=0)
    d_middle = d_out + norm_back(d_hid_b * norm_ffn, normed_b, inv_b)
    d_middle_b = d_middle.astype(jnp.bfloat16)
    g_out = contract_rows(attn, d_middle_b)
    d_attn = contract_cols(d_middle_b, w_out).astype(jnp.bfloat16).reshape(tok_rows, head_cnt, HD)
    prob_full = jnp.exp(scores_of(keys_all) - log_total)
    prob_back = prob_full.astype(jnp.bfloat16)
    d_prob = jnp.einsum("qhd,kd->hqk", d_attn, keys_all[:, HD:], preferred_element_type=jnp.float32)
    delta = jnp.sum(prob_full * d_prob, axis=-1, keepdims=True)
    d_score = (prob_full * (d_prob - delta)).astype(jnp.bfloat16)
    d_query = (
        jnp.einsum("hqk,kd->qhd", d_score, keys_all[:, :HD], preferred_element_type=jnp.float32)
        * scale
    )
    d_key = jnp.einsum("hqk,qhd->kd", d_score, query, preferred_element_type=jnp.float32) * scale
    d_value = jnp.einsum("hqk,qhd->kd", prob_back, d_attn, preferred_element_type=jnp.float32)
    d_shared = jnp.concatenate([d_key, d_value], axis=1)
    local_grad = d_shared[rim_rows:]
    for offset in range(1, rim_shards + 1):
        piece = d_shared[(rim_shards - offset) * tok_rows : (rim_shards - offset + 1) * tok_rows]
        local_grad = local_grad + shifted(piece.astype(jnp.bfloat16), "seq", -offset).astype(
            piece.dtype
        )
    d_query_b = (
        unrotate(d_query, cos_table[:, None, :], sin_table[:, None, :])
        .reshape(tok_rows, head_cnt * HD)
        .astype(jnp.bfloat16)
    )
    g_query = contract_rows(hid_a, d_query_b)
    part_hid_a, summed_kv = (
        lax.psum(contract_cols(d_query_b, w_query).astype(jnp.bfloat16), "mp").astype(jnp.float32),
        lax.psum(local_grad.astype(jnp.bfloat16), "mp").astype(jnp.float32),
    )
    shared_grad = summed_kv + next_kv_grad.astype(jnp.float32)
    d_keyval = jnp.concatenate(
        [unrotate(shared_grad[:, :HD], cos_table, sin_table), shared_grad[:, HD:]], axis=1
    ).astype(jnp.bfloat16)
    g_keyval = contract_rows(hid_a, d_keyval)
    d_hid_a = part_hid_a + contract_cols(d_keyval, w_keyval)
    g_gain_a = jnp.sum(d_hid_a * normed_a, axis=0)
    input_grad = (d_middle + norm_back(d_hid_a * norm_attn, normed_a, inv_a)).astype(jnp.bfloat16)
    s_query, s_keyval, s_gate, s_up, s_gain_a, s_gain_b = (
        lax.psum_scatter(g_query, "seq", scatter_dimension=0, tiled=True),
        lax.psum_scatter(g_keyval, "seq", scatter_dimension=0, tiled=True),
        lax.psum_scatter(g_gate, "seq", scatter_dimension=0, tiled=True),
        lax.psum_scatter(g_up, "seq", scatter_dimension=0, tiled=True),
        lax.psum_scatter(g_gain_a, "seq", scatter_dimension=0, tiled=True),
        lax.psum_scatter(g_gain_b, "seq", scatter_dimension=0, tiled=True),
    )
    s_out, s_down = (
        lax.psum_scatter(g_out, "seq", scatter_dimension=1, tiled=True),
        lax.psum_scatter(g_down, "seq", scatter_dimension=1, tiled=True),
    )
    return (
        mixed,
        input_grad,
        shared,
        shared_grad,
        s_gain_a,
        s_gain_b,
        s_query,
        s_keyval,
        s_out,
        s_gate,
        s_up,
        s_down,
    )


def solution(mesh):
    placed = (
        P("seq", None),
        P("seq", None),
        P("seq", None),
        P(),
        P(),
        P(),
        P(),
        P(None, "mp"),
        P(),
        P("mp", None),
        P(None, "mp"),
        P(None, "mp"),
        P("mp", None),
    )
    return jax.shard_map(
        shards,
        mesh=mesh,
        in_specs=placed,
        out_specs=(
            P("seq", None),
            P("seq", None),
            P("seq", None),
            P("seq", None),
            P("seq"),
            P("seq"),
            P("seq", "mp"),
            P("seq", None),
            P("mp", "seq"),
            P("seq", "mp"),
            P("seq", "mp"),
            P("mp", "seq"),
        ),
        check_vma=False,
    )
```

profile of v0, /device:TPU:0, one launch (start us, length us, event | category | flops | bytes accessed | tf_op | source)
XLA Modules:
  0.0 2145.0 jit_solution(9401706081982269264)
XLA Ops:
  7.3 1.6 fusion.32
  10.7 1.9 fusion.76
  13.0 1.9 collective-permute-start.1
  15.0 4.5 collective-permute-start
  21.1 3.5 convolution_bitcast_fusion
  27.9 1.5 fusion.86
  30.2 1.8 copy-done.1
  32.0 1.3 fusion.35
  34.2 2.2 convolution_convert_fusion.3
  37.0 13.0 convolution_convert_fusion
  50.0 36.1 %all-reduce.8.cloned.1.call-done = bf16[256,2048]{1,0:T(8,128)(2,1)} async-done(((bf16[256,2048]{1,0:T(8,128)(2,1)}), bf16[256,2048]{1,0:T(8,128)(2,1)}) %all-reduce.8.cloned.1.call-update) | async-done | bytes 1048592 | tf_op jit(solution)/shard_map/psum | solution.py:146
  86.1 1.7 multiply_reduce_fusion
  89.0 7.0 fusion.87
  97.0 5.5 fusion.15
  102.4 6.5 fusion.88
  109.0 8.5 fusion.18
  117.8 1.3 log_add_fusion
  119.1 8.8 convolution_convert_fusion.1
  127.9 37.3 %all-reduce.10.cloned.1.call-done = bf16[256,2048]{1,0:T(8,128)(2,1)} async-done(((bf16[256,2048]{1,0:T(8,128)(2,1)}), bf16[256,2048]{1,0:T(8,128)(2,1)}) %all-reduce.10.cloned.1.call-update) | async-done | bytes 1048592 | tf_op jit(solution)/shard_map/psum | solution.py:168
  165.3 2.9 fusion.24
  168.8 4.6 convolution_convert_fusion.4
  173.4 2.0 copy.108
  175.4 5.0 fusion.36
  180.4 4.8 fusion
  185.3 2.1 fusion.2
  187.4 3.1 fusion.39
  190.5 1.4 fusion.34
  193.5 2.0 copy.88
  196.6 1.3 collective-permute-start.2
  197.9 1.5 collective-permute-start.3
  199.5 4.7 convolution_convert_fusion.2
  204.1 2.2 collective-permute-done.3
  208.1 75.9 %all-reduce.12.cloned.1.call-done = (bf16[256,2048]{1,0:T(8,128)(2,1)}, bf16[256,2048]{1,0:T(8,128)(2,1)}, bf16[256,256]{0,1:T(8,128)(2,1)}) async-done(((bf16[256,2048]{1,0:T(8,128)(2,1)}, bf16[256,2048]{1,0:T(8,128)(2,1)}, bf16[256,256]{0,1:T(8,128)(2,1)}), (bf16[256,2048]{1,0:T(8,128)(2,1)}, bf16[256,2048]{1,0:T(8,128)(2,1)}, bf16[256,256]{0,1:T(8,128)(2,1)})) %all-reduce.12.cloned.1.call-update) | async-done | bytes 2228240 | tf_op jit(solution)/shard_map/psum | solution.py:157
  286.6 2.6 fusion.67
  289.4 7.0 fusion.43
  297.0 5.8 fusion.73
  302.9 13.5 fusion.78
  316.7 12.6 fusion.89
  329.4 12.5 fusion.90
  343.6 1.2 dynamic-slice
  346.3 3.7 fusion.31
  349.9 279.4 %all-reduce.2 = (f32[2048]{0:T(1024)S(1)}, f32[2048]{0:T(1024)S(1)}) all-reduce(f32[2048]{0:T(1024)S(1)} %get-tuple-element.62, f32[2048]{0:T(1024)S(1)} %copy-done.40), channel_id=2, replica_groups=mesh['seq'=64,'mp'=2] {'seq'}, use_global_device_ids=true, to_apply=%region_19.20.clone | all-reduce | flops 4096 | bytes 32768
  630.5 5.5 fusion.30
  636.1 238.3 %reduce-scatter.11.cloned.1.call-done = f32[1024,32]{0,1:T(8,128)} async-done(((f32[1024,2048]{0,1:T(8,128)}), f32[1024,32]{0,1:T(8,128)}) %reduce-scatter.11.cloned.1.call-update) | async-done | bytes 131088 | tf_op jit(solution)/shard_map/reduce_scatter | solution.py:221
  874.4 297.7 %reduce-scatter.7.cloned.1.call-done = f32[32,1024]{1,0:T(8,128)} async-done(((f32[2048,1024]{1,0:T(8,128)}), f32[32,1024]{1,0:T(8,128)}) %reduce-scatter.7.cloned.1.call-update) | async-done | bytes 131088 | tf_op jit(solution)/shard_map/reduce_scatter | solution.py:213
  1172.1 321.7 %reduce-scatter.15.cloned.1.call-done = f32[32,2816]{1,0:T(8,128)} async-done(((f32[2048,2816]{1,0:T(8,128)}), f32[32,2816]{1,0:T(8,128)}) %reduce-scatter.15.cloned.1.call-update) | async-done | bytes 360464 | tf_op jit(solution)/shard_map/reduce_scatter | solution.py:216
  1493.8 322.1 %reduce-scatter.13.cloned.1.call-done = f32[32,2816]{1,0:T(8,128)} async-done(((f32[2048,2816]{1,0:T(8,128)}), f32[32,2816]{1,0:T(8,128)}) %reduce-scatter.13.cloned.1.call-update) | async-done | bytes 360464 | tf_op jit(solution)/shard_map/reduce_scatter | solution.py:215
  1815.9 322.1 %reduce-scatter.17.cloned.1.call-done = f32[2816,32]{0,1:T(8,128)} async-done(((f32[2816,2048]{0,1:T(8,128)}), f32[2816,32]{0,1:T(8,128)}) %reduce-scatter.17.cloned.1.call-update) | async-done | bytes 360464 | tf_op jit(solution)/shard_map/reduce_scatter | solution.py:222
  (193 shorter events, 23.7 us)
Async XLA Ops:
  7.2 3.5 copy-start
  7.2 78.9 %all-reduce.8.cloned.1.call-start = ((), (), s32[]{:S(2)}) async-start(), calls=%async_computation.6 | async-start | bytes 2097152 | tf_op jit(solution)/shard_map/psum | solution.py:146
  7.3 5.7 copy-start.57
  7.3 5.7 copy-start.54
  8.9 12.2 copy-start.2
  8.9 12.2 copy-start.33
  8.9 12.2 copy-start.41
  10.7 9.4 copy-start.50
  12.6 8.5 copy-start.24
  13.0 8.1 copy-start.28
  13.0 8.1 copy-start.30
  13.0 11.7 copy-start.26
  13.0 13.8 collective-permute-start.1
  15.0 11.9 collective-permute-start
  21.0 4.6 copy-start.19
  21.1 4.5 copy-start.21
  27.9 152.5 %copy-start.15 = (bf16[768,256]{0,1:T(8,128)(2,1)}, bf16[768,256]{0,1:T(8,128)(2,1)S(1)}, u32[]{:S(2)}) copy-start(bf16[768,256]{0,1:T(8,128)(2,1)S(1)} %maximum_maximum_fusion) | copy-start | bytes 1179652
  36.5 128.8 %all-reduce.10.cloned.1.call-start = ((), (), s32[]{:S(2)}) async-start(), calls=%async_computation.7 | async-start | bytes 2097152 | tf_op jit(solution)/shard_map/psum | solution.py:168
  50.0 38.4 %copy-start.34 = (f32[2048]{0:T(1024)S(1)}, f32[2048]{0:T(1024)}, u32[]{:S(2)}) copy-start(f32[2048]{0:T(1024)} %param.19) | copy-start | bytes 24580
  88.4 7.6 slice-start.2
  89.0 7.0 copy-start.4
  89.0 7.0 copy-start.18
  89.0 7.1 slice-start.3
  89.0 8.0 slice-start.4
  97.0 12.0 copy-start.14
  102.4 6.6 copy-start.17
  117.6 166.5 %all-reduce.12.cloned.1.call-start = ((), (), s32[]{:S(2)}) async-start(), calls=%async_computation.14 | async-start | bytes 4456448 | tf_op jit(solution)/shard_map/psum | solution.py:157
  165.3 3.5 copy-start.5
  165.3 3.5 copy-start.7
  165.3 3.5 copy-start.45
  175.4 5.0 copy-start.11
  175.4 5.0 copy-start.37
  175.4 9.8 slice-start
  180.4 4.9 slice-start.1
  196.6 7.5 collective-permute-start.2
  197.9 8.4 collective-permute-start.3
  199.5 6.9 copy-start.13
  207.1 429.0 %reduce-scatter.9.cloned.1.call-start = ((), (), s32[]{:S(2)}) async-start(), calls=%async_computation.9 | async-start | bytes 2129920 | tf_op jit(solution)/shard_map/reduce_scatter | solution.py:214
  285.9 3.3 copy-start.35
  289.3 585.1 %reduce-scatter.11.cloned.1.call-start = ((), (), s32[]{:S(2)}) async-start(), calls=%async_computation.10 | async-start | bytes 8519680 | tf_op jit(solution)/shard_map/reduce_scatter | solution.py:221
  296.4 875.8 %reduce-scatter.7.cloned.1.call-start = ((), (), s32[]{:S(2)}) async-start(), calls=%async_computation.8 | async-start | bytes 8519680 | tf_op jit(solution)/shard_map/reduce_scatter | solution.py:213
  302.9 1190.9 %reduce-scatter.15.cloned.1.call-start = ((), (), s32[]{:S(2)}) async-start(), calls=%async_computation.12 | async-start | bytes 23429120 | tf_op jit(solution)/shard_map/reduce_scatter | solution.py:216
  316.4 1499.4 %reduce-scatter.13.cloned.1.call-start = ((), (), s32[]{:S(2)}) async-start(), calls=%async_computation.11 | async-start | bytes 23429120 | tf_op jit(solution)/shard_map/reduce_scatter | solution.py:215
  329.3 1808.7 %reduce-scatter.17.cloned.1.call-start = ((), (), s32[]{:S(2)}) async-start(), calls=%async_computation.13 | async-start | bytes 23429120 | tf_op jit(solution)/shard_map/reduce_scatter | solution.py:222
  346.3 3.7 copy-start.40
  346.3 284.3 %copy-start.43 = (f32[256]{0:T(256)S(1)}, f32[256]{0:T(256)}, u32[]{:S(2)}) copy-start(f32[256]{0:T(256)} %copy-done.41) | copy-start | bytes 3076
  346.3 284.3 %copy-start.47 = (f32[256]{0:T(256)S(1)}, f32[256]{0:T(256)}, u32[]{:S(2)}) copy-start(f32[256]{0:T(256)} %copy-done.44) | copy-start | bytes 3076
  346.3 284.3 %copy-start.53 = (f32[256]{0:T(256)S(1)}, f32[256]{0:T(256)}, u32[]{:S(2)}) copy-start(f32[256]{0:T(256)} %copy-done.51) | copy-start | bytes 3076
  (29 other events, 52.3 us)
Sparse Core Ops, SparseCore 0:
  36.6 49.4 all-reduce.7
  117.7 47.5 all-reduce.9
  207.2 76.7 all-reduce.11
  289.4 287.1 reduce-scatter.8
  579.4 294.9 reduce-scatter.10
  877.2 294.8 reduce-scatter.6
  1175.1 318.6 reduce-scatter.14
  1496.8 319.0 reduce-scatter.12
  1818.9 319.0 reduce-scatter.16
where the time goes:
time: 2150 us; the launch traced here: 2140 us
  waiting for transfers between devices  1650 us (77%)
  blocking collectives  279 us (13%)
  matrix products  141 us (7%)
  other arithmetic  27.4 us (1%)
    reduce_scatter x1, waiting for transfers between devices, shards(): lax.psum_scatter(g_down, 'seq', scatter_dimension=1, tiled=True)  322 us
    reduce_scatter x1, waiting for transfers between devices, shards(): lax.psum_scatter(g_gate, 'seq', scatter_dimension=0, tiled=True)  322 us
    reduce_scatter x1, waiting for transfers between devices, shards(): lax.psum_scatter(g_up, 'seq', scatter_dimension=0, tiled=True)  322 us
    reduce_scatter x1, waiting for transfers between devices, shards(): lax.psum_scatter(g_query, 'seq', scatter_dimension=0, tiled=True)  298 us
    unnamed x1, blocking collectives  279 us
    reduce_scatter x1, waiting for transfers between devices, shards(): lax.psum_scatter(g_out, 'seq', scatter_dimension=1, tiled=True)  238 us
    psum x1, waiting for transfers between devices, shards(): lax.psum(jnp.dot(act, w_down, preferred_element_type=jnp.float32).astype(...  75.9 us
    dot_general x6, matrix products, contract_rows(): lax.dot_general(left, right, (((0,), (0,)), ((), ())), preferred_element_...  54 us
  transfers between devices with their start and end apart: 13, of which 9 were waited for; matrix products, arithmetic and copies ran while one was open for 5% of the time, Pallas kernels for 0%

commit v1 on v0

v1 whole, which is shorter than its diff:
```python
import jax
import jax.numpy as jnp
from jax import lax
from jax.sharding import Mesh, PartitionSpec as P

HD = 128
WINDOW = 512
EPSILON = 1e-05
THETA = 10000.0
MASKED = -1e30
SEQ = ("xl", "y", "z", "c")
SIZES = {"xl": 2, "y": 4, "z": 4, "c": 2, "mp": 2}
BF = jnp.bfloat16
F32 = jnp.float32


def step_to(value, axis, steps):
    count = SIZES[axis]
    return lax.ppermute(value, axis, [(i, (i + steps) % count) for i in range(count)])


def shifted(value, steps):
    count = 64
    first, last = max(0, -steps), min(count, count - steps)
    return lax.ppermute(value, SEQ, [(i, i + steps) for i in range(first, last)])


def rounded(value):
    return lax.optimization_barrier(value.astype(BF)).astype(F32)


def mm(left, right):
    return jnp.dot(left, right, preferred_element_type=F32)


def contract_cols(left, right):
    return lax.dot_general(left, right, (((1,), (1,)), ((), ())), preferred_element_type=F32)


def pick(stack, index):
    return lax.dynamic_index_in_dim(stack, index, 0, keepdims=False)


def mp_sum(value):
    own = value.astype(BF)
    return own.astype(F32) + step_to(own, "mp", 1).astype(F32)


def token_facts(token_idx, seq_lengths, pad_counts):
    ends = jnp.cumsum(seq_lengths)
    which = jnp.sum((token_idx[:, None] >= ends[None, :]).astype(jnp.int32), axis=1)
    member = which[:, None] == jnp.arange(seq_lengths.shape[0], dtype=jnp.int32)[None, :]
    begin = jnp.sum(jnp.where(member, (ends - seq_lengths)[None, :], 0), axis=1)
    live = jnp.sum(jnp.where(member, (seq_lengths - pad_counts)[None, :], 0), axis=1)
    place = token_idx - begin
    return (jnp.where(token_idx >= 0, which, -1), place, place < live)


def rotation(place):
    half = HD // 2
    freqs = jnp.exp(-jnp.log(THETA) * jnp.arange(half, dtype=F32) * 2.0 / HD)
    angle = place.astype(F32)[:, None] * freqs[None, :]
    return (jnp.cos(angle), jnp.sin(angle))


def rotate(value, cos_table, sin_table):
    half = value.shape[-1] // 2
    low, high = value[..., :half], value[..., half:]
    return jnp.concatenate(
        [low * cos_table - high * sin_table, high * cos_table + low * sin_table], axis=-1
    )


def unrotate(value, cos_table, sin_table):
    return rotate(value, cos_table, -sin_table)


def norm_back(d_normed, normed, inverse):
    return inverse * (d_normed - normed * jnp.mean(d_normed * normed, axis=-1, keepdims=True))


def by_core(value, order):
    rows = value.T.reshape(2, 4, 4, 2, 32, value.shape[0])
    return rows.transpose((3,) + order + (4, 5)).reshape(2, 1024, value.shape[0])


def core_tokens(value, order):
    c = lax.axis_index("c")
    halves = by_core(value, order)
    return jnp.concatenate([pick(halves, c), step_to(pick(halves, 1 - c), "c", 1)], axis=1)


def ring_gather(value, axis):
    before, after = step_to(value, axis, 1), step_to(value, axis, -1)
    half = value.shape[0] // 2
    far_a, far_b = step_to(before[:half], axis, 1), step_to(after[half:], axis, -1)
    return [value, before, jnp.concatenate([far_a, far_b], axis=0), after]


def deal(value, axis):
    tokens, width = value.shape
    i = lax.axis_index(axis)
    parts = value.reshape(tokens, 4, width // 4).transpose(1, 0, 2)
    out = [pick(parts, i)]
    for k in (1, 2, 3):
        out.append(step_to(pick(parts, (i + k) % 4), axis, k))
    return [jnp.concatenate([p, step_to(p, "c", 1)], axis=0) for p in out]


def ring_sum(value, axis):
    i = lax.axis_index(axis)
    parts = value.reshape(4, value.shape[0] // 4, value.shape[1])
    half = parts.shape[1] // 2
    far = pick(parts, (i + 2) % 4).astype(BF)
    from_low, from_high = step_to(far[:half], axis, 1), step_to(far[half:], axis, -1)
    up, down = pick(parts, (i + 1) % 4), pick(parts, (i + 3) % 4)
    up = jnp.concatenate([up[:half] + from_low.astype(F32), up[half:]], axis=0).astype(BF)
    down = jnp.concatenate([down[:half], down[half:] + from_high.astype(F32)], axis=0).astype(BF)
    low, high = step_to(up, axis, 1), step_to(down, axis, -1)
    return pick(parts, i) + low.astype(F32) + high.astype(F32)


def pair_sum(value):
    xl = lax.axis_index("xl")
    own = lax.dynamic_index_in_dim(value, xl, 1, keepdims=False)
    other = lax.dynamic_index_in_dim(value, 1 - xl, 1, keepdims=False).astype(BF)
    return own + step_to(other, "xl", 1).astype(F32)


def undeal(value, axis):
    i = lax.axis_index(axis)
    value = value.astype(BF)
    got = [pick(value, i)]
    for k in (1, 2, 3):
        got.append(step_to(pick(value, (i + k) % 4), axis, k))
    stack = jnp.stack(got)
    return jnp.concatenate([pick(stack, (i - part) % 4) for part in range(4)], axis=1)


def shards(
    tokens,
    cotangent,
    next_kv_grad,
    seq_lengths,
    pad_counts,
    norm_attn,
    norm_ffn,
    w_query,
    w_keyval,
    w_out,
    w_gate,
    w_up,
    w_down,
):
    tok_rows = tokens.shape[0]
    rim_shards = (WINDOW + tok_rows - 1) // tok_rows
    rim_rows = rim_shards * tok_rows
    place_in_seq = lax.axis_index(SEQ)
    first_row = place_in_seq * tok_rows
    own_idx = first_row + jnp.arange(tok_rows, dtype=jnp.int32)
    key_idx = first_row - rim_rows + jnp.arange(rim_rows + tok_rows, dtype=jnp.int32)
    seq_q, place_q, real_q = token_facts(own_idx, seq_lengths, pad_counts)
    seq_k, place_k, real_k = token_facts(key_idx, seq_lengths, pad_counts)
    allowed = (
        (seq_q[:, None] == seq_k[None, :])
        & (key_idx[None, :] <= own_idx[:, None])
        & (own_idx[:, None] - key_idx[None, :] < WINDOW)
        & (real_k[None, :] | (key_idx[None, :] == own_idx[:, None]))
    )
    cos_table, sin_table = rotation(place_q)
    head_cnt = w_query.shape[1] // HD
    scale = HD ** (-0.5)
    yzx, zyx = (1, 2, 0), (2, 1, 0)

    cot_all = lax.all_gather(core_tokens(cotangent, zyx), "y")

    x_full = tokens.astype(F32)
    inv_a = lax.rsqrt(jnp.mean(x_full * x_full, axis=-1, keepdims=True) + EPSILON)
    normed_a = x_full * inv_a
    hid_a = (normed_a * norm_attn).astype(BF)
    query = mm(hid_a, w_query).reshape(tok_rows, head_cnt, HD)
    query = rotate(query, cos_table[:, None, :], sin_table[:, None, :]).astype(BF)
    keyval = mm(hid_a, w_keyval)
    shared = jnp.concatenate(
        [rotate(keyval[:, :HD], cos_table, sin_table), keyval[:, HD:]], axis=1
    ).astype(BF)
    rim_pieces = [shifted(shared, offset) for offset in range(rim_shards, 0, -1)]
    keys_all = jnp.concatenate(rim_pieces + [shared], axis=0)

    def scores_of(key_rows):
        scores = (
            jnp.einsum("qhd,kd->hqk", query, key_rows[:, :HD], preferred_element_type=F32) * scale
        )
        return jnp.where(allowed[None], scores, MASKED)

    scores = scores_of(keys_all)
    row_max = jnp.max(scores, axis=-1, keepdims=True)
    exps = jnp.exp(scores - row_max)
    row_total = jnp.sum(exps, axis=-1, keepdims=True)
    prob = (exps / row_total).astype(BF)
    log_total = row_max + jnp.log(row_total)
    attn = jnp.einsum("hqk,kd->qhd", prob, keys_all[:, HD:], preferred_element_type=F32)
    attn = attn.reshape(tok_rows, head_cnt * HD).astype(BF)
    middle = x_full + mp_sum(mm(attn, w_out))
    inv_b = lax.rsqrt(jnp.mean(middle * middle, axis=-1, keepdims=True) + EPSILON)
    normed_b = middle * inv_b
    hid_b = (normed_b * norm_ffn).astype(BF)
    hid_b_all = ring_gather(core_tokens(hid_b, yzx), "z")
    gate = mm(hid_b, w_gate)
    upval = mm(hid_b, w_up)
    sigm = jax.nn.sigmoid(gate)
    act = (gate * sigm * upval).astype(BF)
    d_act = rounded(contract_cols(cotangent, w_down))
    d_gate = (d_act * upval * sigm * (1.0 + gate * (1.0 - sigm))).astype(BF)
    d_up = (d_act * gate * sigm).astype(BF)
    d_hid_b = mp_sum(contract_cols(d_gate, w_gate) + contract_cols(d_up, w_up))

    d_gu_parts = deal(jnp.concatenate([d_gate, d_up], axis=1), "z")
    act_parts = deal(act, "y")
    y = lax.axis_index("y")

    mixed = (middle + mp_sum(mm(act, w_down))).astype(BF)

    g_gu = sum(mm(a, b) for a, b in zip(hid_b_all, d_gu_parts))
    g_down = sum(mm(pick(cot_all, (y - k) % 4), act_parts[k]) for k in range(4))

    d_out = cotangent.astype(F32)
    d_middle = d_out + norm_back(d_hid_b * norm_ffn, normed_b, inv_b)
    d_middle_b = d_middle.astype(BF)
    d_attn = contract_cols(d_middle_b, w_out).astype(BF).reshape(tok_rows, head_cnt, HD)
    attn_pair = jnp.concatenate([attn, step_to(attn, "c", 1)], axis=0)
    g_out = mm(core_tokens(d_middle_b, yzx), attn_pair)

    prob_full = jnp.exp(scores_of(keys_all) - log_total)
    prob_back = prob_full.astype(BF)
    d_prob = jnp.einsum("qhd,kd->hqk", d_attn, keys_all[:, HD:], preferred_element_type=F32)
    delta = jnp.sum(prob_full * d_prob, axis=-1, keepdims=True)
    d_score = (prob_full * (d_prob - delta)).astype(BF)
    d_query = (
        jnp.einsum("hqk,kd->qhd", d_score, keys_all[:, :HD], preferred_element_type=F32) * scale
    )
    d_key = jnp.einsum("hqk,qhd->kd", d_score, query, preferred_element_type=F32) * scale
    d_value = jnp.einsum("hqk,qhd->kd", prob_back, d_attn, preferred_element_type=F32)
    d_shared = jnp.concatenate([d_key, d_value], axis=1)
    local_grad = d_shared[rim_rows:]
    for offset in range(1, rim_shards + 1):
        piece = d_shared[(rim_shards - offset) * tok_rows : (rim_shards - offset + 1) * tok_rows]
        local_grad = local_grad + shifted(piece.astype(BF), -offset).astype(F32)
    d_query_b = (
        unrotate(d_query, cos_table[:, None, :], sin_table[:, None, :])
        .reshape(tok_rows, head_cnt * HD)
        .astype(BF)
    )
    hid_a_pair = core_tokens(hid_a, yzx)
    part_hid_a = mp_sum(contract_cols(d_query_b, w_query))
    summed_kv = mp_sum(local_grad)
    shared_grad = summed_kv + next_kv_grad.astype(F32)
    d_keyval = jnp.concatenate(
        [unrotate(shared_grad[:, :HD], cos_table, sin_table), shared_grad[:, HD:]], axis=1
    ).astype(BF)
    d_qkv = jnp.concatenate([d_query_b, d_keyval], axis=1)
    d_qkv = jnp.concatenate([d_qkv, step_to(d_qkv, "c", 1)], axis=0)
    g_qkv = mm(hid_a_pair, d_qkv)

    s_gu = ring_sum(g_gu, "y")
    s_gu = undeal(pair_sum(s_gu.reshape(4, 2, 32, -1)), "z").astype(F32)
    s_gate, s_up = jnp.split(s_gu, 2, axis=1)
    s_down = ring_sum(g_down, "z")
    s_down = undeal(pair_sum(s_down.reshape(4, 2, 32, -1)), "y").astype(F32).T
    s_out = ring_sum(ring_sum(g_out, "y"), "z")
    s_out = pair_sum(s_out.reshape(1, 2, 32, -1))[0].T
    s_qkv = ring_sum(ring_sum(g_qkv, "y"), "z")
    s_qkv = pair_sum(s_qkv.reshape(1, 2, 32, -1))[0]
    s_query, s_keyval = s_qkv[:, : head_cnt * HD], s_qkv[:, head_cnt * HD :]

    d_hid_a = part_hid_a + contract_cols(d_keyval, w_keyval)
    input_grad = (d_middle + norm_back(d_hid_a * norm_attn, normed_a, inv_a)).astype(BF)

    mine = place_in_seq * 32

    def rows(array):
        return lax.dynamic_slice_in_dim(array, mine, 32, 0).astype(F32)

    gain_b = jnp.sum(rows(w_gate) * s_gate, axis=1) + jnp.sum(rows(w_up) * s_up, axis=1)
    gain_a = jnp.sum(rows(w_query) * s_query, axis=1)
    gains = jnp.stack([gain_a, gain_b])
    gains = gains + step_to(gains, "mp", 1)
    gain_kv = jnp.sum(rows(w_keyval) * s_keyval, axis=1)
    s_gain_a = (gains[0] + gain_kv) / lax.dynamic_slice_in_dim(norm_attn, mine, 32, 0)
    s_gain_b = gains[1] / lax.dynamic_slice_in_dim(norm_ffn, mine, 32, 0)
    return (
        mixed,
        input_grad,
        shared,
        shared_grad,
        s_gain_a,
        s_gain_b,
        s_query,
        s_keyval,
        s_out,
        s_gate,
        s_up,
        s_down,
    )


def solution(mesh):
    fine = Mesh(mesh.devices.reshape(2, 4, 4, 2, 2), SEQ + ("mp",))
    rows = P(SEQ, None)
    placed = (
        rows,
        rows,
        rows,
        P(),
        P(),
        P(),
        P(),
        P(None, "mp"),
        P(),
        P("mp", None),
        P(None, "mp"),
        P(None, "mp"),
        P("mp", None),
    )
    return jax.shard_map(
        shards,
        mesh=fine,
        in_specs=placed,
        out_specs=(
            rows,
            rows,
            rows,
            rows,
            P(SEQ),
            P(SEQ),
            P(SEQ, "mp"),
            rows,
            P("mp", SEQ),
            P(SEQ, "mp"),
            P(SEQ, "mp"),
            P("mp", SEQ),
        ),
        check_vma=False,
    )
```

time: 2150 us -> 468 us (0.22)
  waiting for transfers between devices: 1650 us -> 135 us
  blocking collectives: 279 us -> 0 us
  starting transfers between devices: 10.5 us -> 79.4 us
  local copies, waits for them, and re-layouts: 17.2 us -> 79.8 us
  matrix products: 141 us -> 100 us
  other arithmetic: 27.4 us -> 49.2 us
    reduce_scatter x6 -> x0, waiting for transfers between devices: 1500 us -> none  [the longest x1 322 us: shards(): lax.psum_scatter(g_down, 'seq', scatter_dimension=1, tiled=True)]
    unnamed x1 -> x0, blocking collectives: 279 us -> none
    psum x3 -> x0, waiting for transfers between devices: 149 us -> none  [the longest x1 75.9 us: shards(): lax.psum(jnp.dot(act, w_down, preferred_element_type=jnp.float32).astype(...]
    ppermute x4 -> x68, waiting for transfers between devices: 2.24 us -> 135 us  [the longest x64 135 us: step_to(): lax.ppermute(value, axis, [(i, (i + steps) % count) for i in range(count)])]
    ppermute x4 -> x68, starting transfers between devices: 9.28 us -> 79.4 us  [the longest x64 70.3 us: step_to(): lax.ppermute(value, axis, [(i, (i + steps) % count) for i in range(count)])]
    dot_general x14 -> x18, matrix products: 91 us -> 62.3 us  [the longest x16 59.8 us: mm(): return jnp.dot(left, right, preferred_element_type=F32)]
  transfers between devices with their start and end apart: 13 -> 69, of which waited for: 9 -> 31; matrix products, arithmetic and copies ran while one was open for 5% -> 44% of each run, Pallas kernels for 0% -> 0%
where the time goes in v1:
time: 468 us; the launch traced here: 460 us
  waiting for transfers between devices  135 us (29%)
  matrix products  100 us (21%)
  local copies, waits for them, and re-layouts  79.8 us (17%)
  starting transfers between devices  79.4 us (17%)
  other arithmetic  49.2 us (11%)
  between operations  16.2 us (3%)
    ppermute x64, waiting for transfers between devices, step_to(): lax.ppermute(value, axis, [(i, (i + steps) % count) for i in range(count)])  135 us
    ppermute x64, starting transfers between devices, step_to(): lax.ppermute(value, axis, [(i, (i + steps) % count) for i in range(count)])  70.3 us
    dot_general x16, matrix products, mm(): return jnp.dot(left, right, preferred_element_type=F32)  59.8 us
    dot_general x6, matrix products, contract_cols(): lax.dot_general(left, right, (((1,), (1,)), ((), ())), preferred_element_...  29.4 us
    unnamed x168, local copies, waits for them, and re-layouts  22 us
    another operation x1, local copies, waits for them, and re-layouts  11.6 us
  transfers between devices with their start and end apart: 69, of which 31 were waited for; matrix products, arithmetic and copies ran while one was open for 44% of the time, Pallas kernels for 0%

profile of v1, /device:TPU:0, one launch (start us, length us, event | category | flops | bytes accessed | tf_op | source)
XLA Modules:
  0.0 459.8 jit_solution(7880912701918539218)
XLA Ops:
  16.9 4.6 collective-permute-start
  24.9 3.5 convolution_bitcast_fusion
  41.9 3.6 collective-permute-start.2
  45.5 8.7 %convolution_convert_fusion = bf16[256,2816]{1,0:T(8,128)(2,1)} fusion(bf16[256,2048]{1,0:T(8,128)(2,1)S(1)} %copy-done.15, bf16[2816,2048]{1,0:T(8,128)(2,1)S(1)} %bitcast.443), kind=kOutput, calls=%fused_computation.12 | convolution fusion | flops 2953510912 | bytes 14024704 | tf_op jit(solution)/shard_map/dot_general | solution.py:37
  62.1 7.2 %collective-permute-done.2 = bf16[256,2048]{1,0:T(8,128)(2,1)S(1)} collective-permute-done((bf16[256,2048]{1,0:T(8,128)(2,1)S(1)}, bf16[256,2048]{1,0:T(8,128)(2,1)S(1)}, u32[]{:S(2)}, u32[]{:S(2)}) %collective-permute-start.2) | collective-permute-done | bytes 1048608 | tf_op jit(solution)/shard_map/ppermute | solution.py:19
  70.5 7.0 %fusion.198 = f32[256,2816]{1,0:T(8,128)S(1)} fusion(bf16[256,2048]{1,0:T(8,128)(2,1)S(1)} %multiply_convert_fusion.1, bf16[2048,2816]{1,0:T(8,128)(2,1)} %param.23), kind=kOutput, calls=%fused_computation.386 | convolution fusion | flops 2952790016 | bytes 15466496 | tf_op jit(solution)/shard_map/dot_general | solution.py:33
  77.6 9.4 %fusion.14 = (bf16[256,2816]{1,0:T(8,128)(2,1)S(1)}, bf16[256,2816]{1,0:T(8,128)(2,1)}, bf16[256,2816]{1,0:T(8,128)(2,1)S(1)}) fusion(bf16[256,2816]{1,0:T(8,128)(2,1)S(1)} %copy-done.69, f32[256,2816]{1,0:T(8,128)S(1)} %fusion.198, bf16[256,2048]{1,0:T(8,128)(2,1)S(1)} %multiply_convert_fusion.1, bf16[2048,2816]{1,0:T(8,128)(2,1)} %param.24), kind=kOutput, calls=%fused_computation.26 | convolution fusion | flops 2965045248 | bytes 21233664 | tf_op jit(solution)/shard_map/dot_general | solution.py:33
  87.0 6.2 %fusion.199 = f32[256,2048]{1,0:T(8,128)S(1)} fusion(bf16[256,2816]{1,0:T(8,128)(2,1)S(1)} %get-tuple-element.64, bf16[2048,2816]{1,0:T(8,128)(2,1)} %param.23), kind=kOutput, calls=%fused_computation.387 | convolution fusion | flops 2952790016 | bytes 15073280 | tf_op jit(solution)/shard_map/dot_general | solution.py:37
  94.9 8.5 %fusion.17 = bf16[256,2048]{1,0:T(8,128)(2,1)} fusion(f32[256,2048]{1,0:T(8,128)S(1)} %fusion.199, bf16[256,2816]{1,0:T(8,128)(2,1)S(1)} %get-tuple-element.70, bf16[2048,2816]{1,0:T(8,128)(2,1)} %param.24), kind=kOutput, calls=%fused_computation.34 | convolution fusion | flops 2953838592 | bytes 16121856 | tf_op jit(solution)/shard_map/dot_general | solution.py:37
  103.4 3.0 collective-permute-start.4
  111.3 6.1 %reshape.520 = bf16[256,4,1408]{2,1,0:T(4,128)(2,1)} reshape(bf16[256,5632]{1,0:T(8,128)(2,1)} %pad_maximum_fusion) | data formatting | bytes 5767168 | tf_op jit(solution)/shard_map/reshape | solution.py:103
  117.4 11.6 %constant_dynamic-slice_fusion.8 = (bf16[256,1,1408]{2,1,0:T(2,128)(2,1)}, bf16[256,1,1408]{2,1,0:T(2,128)(2,1)}, bf16[256,1,1408]{2,1,0:T(2,128)(2,1)S(1)}, bf16[256,1,1408]{2,1,0:T(2,128)(2,1)}) fusion(bf16[256,4,1408]{2,1,0:T(4,128)(2,1)} %reshape.520, s32[]{:T(128)S(6)} %select_n.299, s32[]{:T(128)S(6)} %select_n.297, s32[]{:T(128)S(6)} %select_n.295, ...), kind=kLoop, calls=%fused_computation.342 | loop fusion | bytes 5767184 | tf_op jit(solution)/shard_map/dynamic-slice.2
  130.5 8.5 %convolution_convert_fusion.1 = bf16[256,2048]{1,0:T(8,128)(2,1)} fusion(bf16[256,2816]{1,0:T(8,128)(2,1)S(1)} %copy-done.27, bf16[2816,2048]{1,0:T(8,128)(2,1)} %param.25), kind=kOutput, calls=%fused_computation.35 | convolution fusion | flops 2953314304 | bytes 14024704 | tf_op jit(solution)/shard_map/dot_general | solution.py:33
  151.9 5.7 %fusion.25 = f32[1024,1408]{1,0:T(8,128)} fusion(bf16[256,1408]{1,0:T(8,128)(2,1)} %collective-permute-done.21, bf16[256,1408]{1,0:T(8,128)(2,1)} %bitcast.376, bf16[1024,256]{1,0:T(8,128)(2,1)} %collective-permute-done.20, bf16[1024,256]{1,0:T(8,128)(2,1)S(1)} %copy-done.13), kind=kOutput, calls=%fused_computation.52 | convolution fusion | flops 1481375744 | bytes 8257536 | tf_op jit(solution)/shard_map/dot_general | solution.py:33
  160.2 8.7 %collective-permute-done.3 = bf16[256,2048]{1,0:T(8,128)(2,1)S(1)} collective-permute-done((bf16[256,2048]{1,0:T(8,128)(2,1)}, bf16[256,2048]{1,0:T(8,128)(2,1)S(1)}, u32[]{:S(2)}, u32[]{:S(2)}) %collective-permute-start.3) | collective-permute-done | bytes 1048608 | tf_op jit(solution)/shard_map/ppermute | solution.py:19
  168.9 5.0 %convert_bitcast_fusion = (bf16[2048,256]{0,1:T(8,128)(2,1)}, f32[256,2048]{1,0:T(8,128)S(1)}, bf16[256,2048]{1,0:T(8,128)(2,1)}) fusion(f32[256]{0:T(256)S(1)} %broadcast_multiply_fusion.1, bf16[256,2048]{1,0:T(8,128)(2,1)S(1)} %collective-permute-done.2, bf16[256,2048]{1,0:T(8,128)(2,1)S(1)} %convolution_convert_fusion.3, ...), kind=kLoop, calls=%fused_computation.194 | loop fusion | flops 11010048 | bytes 12593152 | tf_op jit(solution)/shard_map/transpose | solution.py:83
  176.8 4.2 fusion
  192.4 3.7 convolution_convert_fusion.2
  199.0 3.9 collective-permute-start.26
  205.5 5.2 %collective-permute-done.8 = bf16[256,256]{0,1:T(8,128)(2,1)S(1)} collective-permute-done((bf16[256,256]{0,1:T(8,128)(2,1)S(1)}, bf16[256,256]{0,1:T(8,128)(2,1)S(1)}, u32[]{:S(2)}, u32[]{:S(2)}) %collective-permute-start.8) | collective-permute-done | bytes 131104 | tf_op jit(solution)/shard_map/ppermute | solution.py:19
  215.5 2.8 fusion.64
  218.5 13.5 %collective-permute-done.28 = bf16[256,1408]{1,0:T(8,128)(2,1)} collective-permute-done((bf16[256,1408]{1,0:T(8,128)(2,1)}, bf16[256,1408]{1,0:T(8,128)(2,1)}, u32[]{:S(2)}, u32[]{:S(2)}) %collective-permute-start.28) | collective-permute-done | bytes 720928 | tf_op jit(solution)/shard_map/ppermute | solution.py:19
  232.0 3.2 collective-permute-start.56
  235.2 5.8 %collective-permute-done.26 = bf16[1024,512]{1,0:T(8,128)(2,1)} collective-permute-done((bf16[1024,512]{1,0:T(8,128)(2,1)S(1)}, bf16[1024,512]{1,0:T(8,128)(2,1)}, u32[]{:S(2)}, u32[]{:S(2)}) %collective-permute-start.26) | collective-permute-done | bytes 1048608 | tf_op jit(solution)/shard_map/ppermute | solution.py:19
  241.5 3.4 fusion.36
  246.1 7.9 %collective-permute-done.22 = bf16[1024,512]{1,0:T(8,128)(2,1)S(1)} collective-permute-done((bf16[1024,512]{1,0:T(8,128)(2,1)S(1)}, bf16[1024,512]{1,0:T(8,128)(2,1)S(1)}, u32[]{:S(2)}, u32[]{:S(2)}) %collective-permute-start.22) | collective-permute-done | bytes 1048608 | tf_op jit(solution)/shard_map/ppermute | solution.py:19
  257.3 3.0 fusion.29
  260.4 3.1 collective-permute-done.43
  265.9 8.4 %collective-permute-start.25 = (bf16[512,512]{1,0:T(8,128)(2,1)S(1)}, bf16[512,512]{1,0:T(8,128)(2,1)}, u32[]{:S(2)}, u32[]{:S(2)}) collective-permute-start(bf16[512,512]{1,0:T(8,128)(2,1)S(1)} %slice.418), channel_id=1, source_target_pairs={{0,4},{4,8},{8,12},{12,0},{1,5},{5,9},{9,13},{13,1},{2,6},{6,10},{... | collective-permute-start | bytes 1572872 | tf_op jit(solution)/shard_map/ppermute | solution.py:19
  278.6 9.4 %collective-permute-done.25 = bf16[512,512]{1,0:T(8,128)(2,1)} collective-permute-done((bf16[512,512]{1,0:T(8,128)(2,1)S(1)}, bf16[512,512]{1,0:T(8,128)(2,1)}, u32[]{:S(2)}, u32[]{:S(2)}) %collective-permute-start.25) | collective-permute-done | bytes 524320 | tf_op jit(solution)/shard_map/ppermute | solution.py:19
  288.0 3.5 add_add_fusion
  294.7 3.3 fusion.190
  302.6 3.2 collective-permute-start.49
  311.4 4.8 %collective-permute-done.34 = bf16[128,1408]{1,0:T(8,128)(2,1)S(1)} collective-permute-done((bf16[128,1408]{1,0:T(8,128)(2,1)S(1)}, bf16[128,1408]{1,0:T(8,128)(2,1)S(1)}, u32[]{:S(2)}, u32[]{:S(2)}) %collective-permute-start.34) | collective-permute-done | bytes 360480 | tf_op jit(solution)/shard_map/ppermute | solution.py:19
  330.4 7.6 %collective-permute-done.11 = bf16[128,1280]{1,0:T(8,128)(2,1)S(1)} collective-permute-done((bf16[128,1280]{1,0:T(8,128)(2,1)S(1)}, bf16[128,1280]{1,0:T(8,128)(2,1)S(1)}, u32[]{:S(2)}, u32[]{:S(2)}) %collective-permute-start.11) | collective-permute-done | bytes 327712 | tf_op jit(solution)/shard_map/ppermute | solution.py:19
  340.2 13.2 %collective-permute-done.33 = bf16[256,1408]{1,0:T(8,128)(2,1)S(1)} collective-permute-done((bf16[256,1408]{1,0:T(8,128)(2,1)S(1)}, bf16[256,1408]{1,0:T(8,128)(2,1)S(1)}, u32[]{:S(2)}, u32[]{:S(2)}) %collective-permute-start.33) | collective-permute-done | bytes 720928 | tf_op jit(solution)/shard_map/ppermute | solution.py:19
  357.5 3.7 collective-permute-done.36
  362.1 3.8 collective-permute-done.14
  365.9 3.8 collective-permute-done.12
  372.4 3.0 collective-permute-done.37
  385.3 2.7 collective-permute-done.16
  389.4 3.2 collective-permute-done.19
  399.8 4.7 %reshape.531 = f32[4,256,704]{1,0,2:T(4,128)} reshape(f32[1024,704]{0,1:T(8,128)} %add_add_fusion.1) | data formatting | bytes 5767168 | tf_op jit(solution)/shard_map/reshape | solution.py:112
  409.1 5.6 %constant_dynamic-slice_fusion.3 = (f32[1,256,704]{1,0,2:T(1,128)S(1)}, f32[1,256,704]{1,0,2:T(1,128)S(1)}, f32[1,256,704]{1,0,2:T(1,128)S(1)}) fusion(f32[4,256,704]{1,0,2:T(4,128)} %reshape.531, s32[]{:T(128)S(6)} %select_n.297, s32[]{:T(128)S(6)} %select_n.301, s32[]{:T(128)S(6)} %select_n.295), kind=kLoop, calls=%fused_computation.333 | loop fusion | bytes 4325388 | tf_op jit(solution)/shard_map/jit(dynamic_index_in_dim)/dynamic_slice | solution.py:41
  424.1 2.7 collective-permute-done.60
  432.7 5.0 %collective-permute-done.61 = bf16[256,704]{1,0:T(8,128)(2,1)S(1)} collective-permute-done((bf16[256,704]{1,0:T(8,128)(2,1)S(1)}, bf16[256,704]{1,0:T(8,128)(2,1)S(1)}, u32[]{:S(2)}, u32[]{:S(2)}) %collective-permute-start.61) | collective-permute-done | bytes 360480 | tf_op jit(solution)/shard_map/ppermute | solution.py:19
  439.1 4.5 collective-permute-done.64
  448.2 2.9 collective-permute-done.66
  (430 shorter events, 177.7 us)
Async XLA Ops:
  7.2 385.6 %all-gather.3.cloned.1.call-start = ((), (), s32[]{:S(2)}) async-start(), calls=%async_computation | async-start | bytes 5242880 | tf_op jit(solution)/shard_map/all_gather | solution.py:175
  15.0 17.2 %collective-permute-start.1 = (bf16[256,256]{0,1:T(8,128)(2,1)S(1)}, bf16[256,256]{0,1:T(8,128)(2,1)}, u32[]{:S(2)}, u32[]{:S(2)}) collective-permute-start(bf16[256,256]{0,1:T(8,128)(2,1)S(1)} %pad_maximum_fusion.19), channel_id=1, source_target_pairs={{0,2},{2,4},{4,6},{6,8},{8,10},{10,12},{12,14},{14,16},{16,18},{18... | collective-permute-start | bytes 393224 | tf_op jit(solution)/shard_map/ppermute | solution.py:25
  16.9 15.2 %collective-permute-start = (bf16[256,256]{0,1:T(8,128)(2,1)S(1)}, bf16[256,256]{0,1:T(8,128)(2,1)}, u32[]{:S(2)}, u32[]{:S(2)}) collective-permute-start(bf16[256,256]{0,1:T(8,128)(2,1)S(1)} %pad_maximum_fusion.19), channel_id=1, source_target_pairs={{0,4},{2,6},{4,8},{6,10},{8,12},{10,14},{12,16},{14,18},{16,20},{1... | collective-permute-start | bytes 393224 | tf_op jit(solution)/shard_map/ppermute | solution.py:25
  23.2 36.6 %collective-permute-start.52 = (bf16[1024,256]{1,0:T(8,128)(2,1)}, bf16[1024,256]{1,0:T(8,128)(2,1)}, u32[]{:S(2)}, u32[]{:S(2)}) collective-permute-start(bf16[1024,256]{1,0:T(8,128)(2,1)} %get-tuple-element.98), channel_id=1, source_target_pairs={{0,2},{2,0},{1,3},{3,1},{4,6},{6,4},{5,7},{7,5},{8,10},{10,8},{9,1... | collective-permute-start | bytes 1572872 | tf_op jit(solution)/shard_map/ppermute | solution.py:19
  41.9 27.4 %collective-permute-start.2 = (bf16[256,2048]{1,0:T(8,128)(2,1)S(1)}, bf16[256,2048]{1,0:T(8,128)(2,1)S(1)}, u32[]{:S(2)}, u32[]{:S(2)}) collective-permute-start(bf16[256,2048]{1,0:T(8,128)(2,1)S(1)} %convolution_convert_fusion.3), channel_id=1, source_target_pairs={{0,1},{1,0},{2,3},{3,2},{4,5},{5,4},{6,7},{7,6},{8,9},{9,8},{10,11... | collective-permute-start | bytes 3145736 | tf_op jit(solution)/shard_map/ppermute | solution.py:19
  59.1 152.0 %collective-permute-start.42 = (bf16[256,1024]{0,1:T(8,128)(2,1)}, bf16[256,1024]{0,1:T(8,128)(2,1)}, u32[]{:S(2)}, u32[]{:S(2)}) collective-permute-start(bf16[256,1024]{0,1:T(8,128)(2,1)} %bitcast.445), channel_id=1, source_target_pairs={{0,2},{2,0},{1,3},{3,1},{4,6},{6,4},{5,7},{7,5},{8,10},{10,8},{9,1... | collective-permute-start | bytes 1572872 | tf_op jit(solution)/shard_map/ppermute | solution.py:19
  103.4 54.1 %collective-permute-start.4 = (bf16[256,2048]{1,0:T(8,128)(2,1)}, bf16[256,2048]{1,0:T(8,128)(2,1)}, u32[]{:S(2)}, u32[]{:S(2)}) collective-permute-start(bf16[256,2048]{1,0:T(8,128)(2,1)} %fusion.17), channel_id=1, source_target_pairs={{0,1},{1,0},{2,3},{3,2},{4,5},{5,4},{6,7},{7,6},{8,9},{9,8},{10,11... | collective-permute-start | bytes 3145736 | tf_op jit(solution)/shard_map/ppermute | solution.py:19
  111.1 36.4 %collective-permute-start.20 = (bf16[1024,256]{1,0:T(8,128)(2,1)}, bf16[1024,256]{1,0:T(8,128)(2,1)}, u32[]{:S(2)}, u32[]{:S(2)}) collective-permute-start(bf16[1024,256]{1,0:T(8,128)(2,1)} %get-tuple-element.106), channel_id=1, source_target_pairs={{0,2},{2,0},{1,3},{3,1},{4,6},{6,4},{5,7},{7,5},{8,10},{10,8},{9,1... | collective-permute-start | bytes 1572872 | tf_op jit(solution)/shard_map/ppermute | solution.py:19
  129.9 21.6 %collective-permute-start.21 = (bf16[256,1408]{1,0:T(8,128)(2,1)}, bf16[256,1408]{1,0:T(8,128)(2,1)}, u32[]{:S(2)}, u32[]{:S(2)}) collective-permute-start(bf16[256,1408]{1,0:T(8,128)(2,1)} %bitcast.376), channel_id=1, source_target_pairs={{0,2},{2,0},{1,3},{3,1},{4,6},{6,4},{5,7},{7,5},{8,10},{10,8},{9,1... | collective-permute-start | bytes 2162696 | tf_op jit(solution)/shard_map/ppermute | solution.py:19
  141.6 27.3 %collective-permute-start.3 = (bf16[256,2048]{1,0:T(8,128)(2,1)}, bf16[256,2048]{1,0:T(8,128)(2,1)S(1)}, u32[]{:S(2)}, u32[]{:S(2)}) collective-permute-start(bf16[256,2048]{1,0:T(8,128)(2,1)} %convolution_convert_fusion.1), channel_id=1, source_target_pairs={{0,1},{1,0},{2,3},{3,2},{4,5},{5,4},{6,7},{7,6},{8,9},{9,8},{10,11... | collective-permute-start | bytes 3145736 | tf_op jit(solution)/shard_map/ppermute | solution.py:19
  147.6 65.6 %collective-permute-start.30 = (bf16[256,1408]{1,0:T(8,128)(2,1)}, bf16[256,1408]{1,0:T(8,128)(2,1)}, u32[]{:S(2)}, u32[]{:S(2)}) collective-permute-start(bf16[256,1408]{1,0:T(8,128)(2,1)} %bitcast.373), channel_id=1, source_target_pairs={{0,12},{4,0},{8,4},{12,8},{1,13},{5,1},{9,5},{13,9},{2,14},{6,2},{... | collective-permute-start | bytes 2162696 | tf_op jit(solution)/shard_map/ppermute | solution.py:19
  151.5 63.6 %collective-permute-start.23 = (bf16[256,1408]{1,0:T(8,128)(2,1)}, bf16[256,1408]{1,0:T(8,128)(2,1)}, u32[]{:S(2)}, u32[]{:S(2)}) collective-permute-start(bf16[256,1408]{1,0:T(8,128)(2,1)} %bitcast.375), channel_id=1, source_target_pairs={{0,4},{4,8},{8,12},{12,0},{1,5},{5,9},{9,13},{13,1},{2,6},{6,10},{... | collective-permute-start | bytes 2162696 | tf_op jit(solution)/shard_map/ppermute | solution.py:19
  189.8 9.2 %collective-permute-start.7 = (bf16[256,256]{0,1:T(8,128)(2,1)}, bf16[256,256]{0,1:T(8,128)(2,1)}, u32[]{:S(2)}, u32[]{:S(2)}) collective-permute-start(bf16[256,256]{0,1:T(8,128)(2,1)} %get-tuple-element.122), channel_id=1, source_target_pairs={{4,0},{6,2},{8,4},{10,6},{12,8},{14,10},{16,12},{18,14},{20,16},{2... | collective-permute-start | bytes 393224 | tf_op jit(solution)/shard_map/ppermute | solution.py:25
  191.0 11.8 %collective-permute-start.6 = (bf16[256,256]{0,1:T(8,128)(2,1)}, bf16[256,256]{0,1:T(8,128)(2,1)}, u32[]{:S(2)}, u32[]{:S(2)}) collective-permute-start(bf16[256,256]{0,1:T(8,128)(2,1)} %get-tuple-element.121), channel_id=1, source_target_pairs={{2,0},{4,2},{6,4},{8,6},{10,8},{12,10},{14,12},{16,14},{18,16},{20... | collective-permute-start | bytes 393224 | tf_op jit(solution)/shard_map/ppermute | solution.py:25
  199.0 42.1 %collective-permute-start.26 = (bf16[1024,512]{1,0:T(8,128)(2,1)S(1)}, bf16[1024,512]{1,0:T(8,128)(2,1)}, u32[]{:S(2)}, u32[]{:S(2)}) collective-permute-start(bf16[1024,512]{1,0:T(8,128)(2,1)S(1)} %copy-done.32), channel_id=1, source_target_pairs={{0,12},{4,0},{8,4},{12,8},{1,13},{5,1},{9,5},{13,9},{2,14},{6,2},{... | collective-permute-start | bytes 3145736 | tf_op jit(solution)/shard_map/ppermute | solution.py:19
  211.1 20.9 %collective-permute-start.28 = (bf16[256,1408]{1,0:T(8,128)(2,1)}, bf16[256,1408]{1,0:T(8,128)(2,1)}, u32[]{:S(2)}, u32[]{:S(2)}) collective-permute-start(bf16[256,1408]{1,0:T(8,128)(2,1)} %bitcast.374), channel_id=1, source_target_pairs={{0,8},{4,12},{8,0},{12,4},{1,9},{5,13},{9,1},{13,5},{2,10},{6,14},... | collective-permute-start | bytes 2162696 | tf_op jit(solution)/shard_map/ppermute | solution.py:19
  213.1 22.1 %collective-permute-start.31 = (bf16[256,1408]{1,0:T(8,128)(2,1)}, bf16[256,1408]{1,0:T(8,128)(2,1)}, u32[]{:S(2)}, u32[]{:S(2)}) collective-permute-start(bf16[256,1408]{1,0:T(8,128)(2,1)} %collective-permute-done.30), channel_id=1, source_target_pairs={{0,2},{2,0},{1,3},{3,1},{4,6},{6,4},{5,7},{7,5},{8,10},{10,8},{9,1... | collective-permute-start | bytes 2162696 | tf_op jit(solution)/shard_map/ppermute | solution.py:19
  215.1 38.8 %collective-permute-start.22 = (bf16[1024,512]{1,0:T(8,128)(2,1)S(1)}, bf16[1024,512]{1,0:T(8,128)(2,1)S(1)}, u32[]{:S(2)}, u32[]{:S(2)}) collective-permute-start(bf16[1024,512]{1,0:T(8,128)(2,1)S(1)} %copy-done.32), channel_id=1, source_target_pairs={{0,4},{4,8},{8,12},{12,0},{1,5},{5,9},{9,13},{13,1},{2,6},{6,10},{... | collective-permute-start | bytes 3145736 | tf_op jit(solution)/shard_map/ppermute | solution.py:19
  215.5 40.1 %collective-permute-start.24 = (bf16[256,1408]{1,0:T(8,128)(2,1)}, bf16[256,1408]{1,0:T(8,128)(2,1)S(1)}, u32[]{:S(2)}, u32[]{:S(2)}) collective-permute-start(bf16[256,1408]{1,0:T(8,128)(2,1)} %collective-permute-done.23), channel_id=1, source_target_pairs={{0,2},{2,0},{1,3},{3,1},{4,6},{6,4},{5,7},{7,5},{8,10},{10,8},{9,1... | collective-permute-start | bytes 2162696 | tf_op jit(solution)/shard_map/ppermute | solution.py:19
  232.0 152.1 %collective-permute-start.56 = (bf16[256,704]{0,1:T(8,128)(2,1)}, bf16[256,704]{0,1:T(8,128)(2,1)}, u32[]{:S(2)}, u32[]{:S(2)}) collective-permute-start(bf16[256,704]{0,1:T(8,128)(2,1)} %get-tuple-element.86), channel_id=1, source_target_pairs={{0,32},{16,48},{32,0},{48,16},{1,33},{17,49},{33,1},{49,17},{2,34}... | collective-permute-start | bytes 1081352 | tf_op jit(solution)/shard_map/ppermute | solution.py:19
  235.2 40.6 %collective-permute-start.29 = (bf16[256,1408]{1,0:T(8,128)(2,1)}, bf16[256,1408]{1,0:T(8,128)(2,1)S(1)}, u32[]{:S(2)}, u32[]{:S(2)}) collective-permute-start(bf16[256,1408]{1,0:T(8,128)(2,1)} %collective-permute-done.28), channel_id=1, source_target_pairs={{0,2},{2,0},{1,3},{3,1},{4,6},{6,4},{5,7},{7,5},{8,10},{10,8},{9,1... | collective-permute-start | bytes 2162696 | tf_op jit(solution)/shard_map/ppermute | solution.py:19
  241.0 24.9 %collective-permute-start.5 = (bf16[256,2048]{1,0:T(8,128)(2,1)S(1)}, bf16[256,2048]{1,0:T(8,128)(2,1)S(1)}, u32[]{:S(2)}, u32[]{:S(2)}) collective-permute-start(bf16[256,2048]{1,0:T(8,128)(2,1)S(1)} %convolution_convert_fusion.2), channel_id=1, source_target_pairs={{0,1},{1,0},{2,3},{3,2},{4,5},{5,4},{6,7},{7,6},{8,9},{9,8},{10,11... | collective-permute-start | bytes 3145736 | tf_op jit(solution)/shard_map/ppermute | solution.py:19
  253.9 9.6 %collective-permute-start.43 = (bf16[128,1024]{1,0:T(8,128)(2,1)S(1)}, bf16[128,1024]{1,0:T(8,128)(2,1)S(1)}, u32[]{:S(2)}, u32[]{:S(2)}) collective-permute-start(bf16[128,1024]{1,0:T(8,128)(2,1)S(1)} %get-tuple-element.117), channel_id=1, source_target_pairs={{0,16},{16,32},{32,48},{48,0},{1,17},{17,33},{33,49},{49,1},{2,18}... | collective-permute-start | bytes 786440 | tf_op jit(solution)/shard_map/ppermute | solution.py:19
  263.5 59.7 %collective-permute-start.10 = (bf16[256,1280]{0,1:T(8,128)(2,1)}, bf16[256,1280]{0,1:T(8,128)(2,1)}, u32[]{:S(2)}, u32[]{:S(2)}) collective-permute-start(bf16[256,1280]{0,1:T(8,128)(2,1)} %pad_maximum_fusion.6), channel_id=1, source_target_pairs={{0,2},{2,0},{1,3},{3,1},{4,6},{6,4},{5,7},{7,5},{8,10},{10,8},{9,1... | collective-permute-start | bytes 1966088 | tf_op jit(solution)/shard_map/ppermute | solution.py:19
  263.6 14.2 %collective-permute-start.27 = (bf16[512,512]{1,0:T(8,128)(2,1)S(1)}, bf16[512,512]{1,0:T(8,128)(2,1)S(1)}, u32[]{:S(2)}, u32[]{:S(2)}) collective-permute-start(bf16[512,512]{1,0:T(8,128)(2,1)S(1)} %slice.419), channel_id=1, source_target_pairs={{0,12},{4,0},{8,4},{12,8},{1,13},{5,1},{9,5},{13,9},{2,14},{6,2},{... | collective-permute-start | bytes 1572872 | tf_op jit(solution)/shard_map/ppermute | solution.py:19
  265.9 22.1 %collective-permute-start.25 = (bf16[512,512]{1,0:T(8,128)(2,1)S(1)}, bf16[512,512]{1,0:T(8,128)(2,1)}, u32[]{:S(2)}, u32[]{:S(2)}) collective-permute-start(bf16[512,512]{1,0:T(8,128)(2,1)S(1)} %slice.418), channel_id=1, source_target_pairs={{0,4},{4,8},{8,12},{12,0},{1,5},{5,9},{9,13},{13,1},{2,6},{6,10},{... | collective-permute-start | bytes 1572872 | tf_op jit(solution)/shard_map/ppermute | solution.py:19
  275.8 24.5 %collective-permute-start.46 = (bf16[256,1024]{1,0:T(8,128)(2,1)}, bf16[256,1024]{1,0:T(8,128)(2,1)}, u32[]{:S(2)}, u32[]{:S(2)}) collective-permute-start(bf16[256,1024]{1,0:T(8,128)(2,1)} %pad_maximum_fusion.12), channel_id=1, source_target_pairs={{0,48},{16,0},{32,16},{48,32},{1,49},{17,1},{33,17},{49,33},{2,50}... | collective-permute-start | bytes 1572872 | tf_op jit(solution)/shard_map/ppermute | solution.py:19
  277.8 22.5 %collective-permute-start.44 = (bf16[256,1024]{1,0:T(8,128)(2,1)}, bf16[256,1024]{1,0:T(8,128)(2,1)}, u32[]{:S(2)}, u32[]{:S(2)}) collective-permute-start(bf16[256,1024]{1,0:T(8,128)(2,1)} %pad_maximum_fusion.11), channel_id=1, source_target_pairs={{0,16},{16,32},{32,48},{48,0},{1,17},{17,33},{33,49},{49,1},{2,18}... | collective-permute-start | bytes 1572872 | tf_op jit(solution)/shard_map/ppermute | solution.py:19
  292.6 16.7 %collective-permute-start.32 = (bf16[128,1408]{1,0:T(8,128)(2,1)}, bf16[128,1408]{1,0:T(8,128)(2,1)}, u32[]{:S(2)}, u32[]{:S(2)}) collective-permute-start(bf16[128,1408]{1,0:T(8,128)(2,1)} %get-tuple-element.113), channel_id=1, source_target_pairs={{0,16},{16,32},{32,48},{48,0},{1,17},{17,33},{33,49},{49,1},{2,18}... | collective-permute-start | bytes 1081352 | tf_op jit(solution)/shard_map/ppermute | solution.py:19
  309.2 14.0 %collective-permute-start.9 = (bf16[1024,256]{1,0:T(8,128)(2,1)S(1)}, bf16[1024,256]{1,0:T(8,128)(2,1)S(1)}, u32[]{:S(2)}, u32[]{:S(2)}) collective-permute-start(bf16[1024,256]{1,0:T(8,128)(2,1)S(1)} %get-tuple-element.108), channel_id=1, source_target_pairs={{0,2},{2,0},{1,3},{3,1},{4,6},{6,4},{5,7},{7,5},{8,10},{10,8},{9,1... | collective-permute-start | bytes 1572872 | tf_op jit(solution)/shard_map/ppermute | solution.py:19
  309.3 8.3 %collective-permute-start.50 = (bf16[64,1024]{1,0:T(8,128)(2,1)S(1)}, bf16[64,1024]{1,0:T(8,128)(2,1)S(1)}, u32[]{:S(2)}, u32[]{:S(2)}) collective-permute-start(bf16[64,1024]{1,0:T(8,128)(2,1)S(1)} %pad_maximum_fusion.21), channel_id=1, source_target_pairs={{0,12},{4,0},{8,4},{12,8},{1,13},{5,1},{9,5},{13,9},{2,14},{6,2},{... | collective-permute-start | bytes 393224 | tf_op jit(solution)/shard_map/ppermute | solution.py:19
  317.6 22.6 %collective-permute-start.35 = (bf16[256,1408]{1,0:T(8,128)(2,1)S(1)}, bf16[256,1408]{1,0:T(8,128)(2,1)S(1)}, u32[]{:S(2)}, u32[]{:S(2)}) collective-permute-start(bf16[256,1408]{1,0:T(8,128)(2,1)S(1)} %pad_maximum_fusion.5), channel_id=1, source_target_pairs={{0,48},{16,0},{32,16},{48,32},{1,49},{17,1},{33,17},{49,33},{2,50}... | collective-permute-start | bytes 2162696 | tf_op jit(solution)/shard_map/ppermute | solution.py:19
  326.0 11.9 %collective-permute-start.11 = (bf16[128,1280]{1,0:T(8,128)(2,1)S(1)}, bf16[128,1280]{1,0:T(8,128)(2,1)S(1)}, u32[]{:S(2)}, u32[]{:S(2)}) collective-permute-start(bf16[128,1280]{1,0:T(8,128)(2,1)S(1)} %get-tuple-element.115), channel_id=1, source_target_pairs={{0,16},{16,32},{32,48},{48,0},{1,17},{17,33},{33,49},{49,1},{2,18}... | collective-permute-start | bytes 983048 | tf_op jit(solution)/shard_map/ppermute | solution.py:19
  327.5 12.5 %collective-permute-start.13 = (bf16[128,1280]{1,0:T(8,128)(2,1)S(1)}, bf16[128,1280]{1,0:T(8,128)(2,1)S(1)}, u32[]{:S(2)}, u32[]{:S(2)}) collective-permute-start(bf16[128,1280]{1,0:T(8,128)(2,1)S(1)} %get-tuple-element.116), channel_id=1, source_target_pairs={{0,48},{16,0},{32,16},{48,32},{1,49},{17,1},{33,17},{49,33},{2,50}... | collective-permute-start | bytes 983048 | tf_op jit(solution)/shard_map/ppermute | solution.py:19
  329.4 24.0 %collective-permute-start.33 = (bf16[256,1408]{1,0:T(8,128)(2,1)S(1)}, bf16[256,1408]{1,0:T(8,128)(2,1)S(1)}, u32[]{:S(2)}, u32[]{:S(2)}) collective-permute-start(bf16[256,1408]{1,0:T(8,128)(2,1)S(1)} %pad_maximum_fusion.4), channel_id=1, source_target_pairs={{0,16},{16,32},{32,48},{48,0},{1,17},{17,33},{33,49},{49,1},{2,18}... | collective-permute-start | bytes 2162696 | tf_op jit(solution)/shard_map/ppermute | solution.py:19
  337.9 46.3 %collective-permute-start.54 = (bf16[256,704]{0,1:T(8,128)(2,1)S(1)}, bf16[256,704]{0,1:T(8,128)(2,1)S(1)}, u32[]{:S(2)}, u32[]{:S(2)}) collective-permute-start(bf16[256,704]{0,1:T(8,128)(2,1)S(1)} %copy-done.41), channel_id=1, source_target_pairs={{0,16},{16,32},{32,48},{48,0},{1,17},{17,33},{33,49},{49,1},{2,18}... | collective-permute-start | bytes 1081352 | tf_op jit(solution)/shard_map/ppermute | solution.py:19
  355.3 10.7 %collective-permute-start.14 = (bf16[256,1280]{1,0:T(8,128)(2,1)S(1)}, bf16[256,1280]{1,0:T(8,128)(2,1)S(1)}, u32[]{:S(2)}, u32[]{:S(2)}) collective-permute-start(bf16[256,1280]{1,0:T(8,128)(2,1)S(1)} %pad_maximum_fusion.8), channel_id=1, source_target_pairs={{0,48},{16,0},{32,16},{48,32},{1,49},{17,1},{33,17},{49,33},{2,50}... | collective-permute-start | bytes 1966088 | tf_op jit(solution)/shard_map/ppermute | solution.py:19
  356.4 13.3 %collective-permute-start.12 = (bf16[256,1280]{1,0:T(8,128)(2,1)S(1)}, bf16[256,1280]{1,0:T(8,128)(2,1)S(1)}, u32[]{:S(2)}, u32[]{:S(2)}) collective-permute-start(bf16[256,1280]{1,0:T(8,128)(2,1)S(1)} %pad_maximum_fusion.7), channel_id=1, source_target_pairs={{0,16},{16,32},{32,48},{48,0},{1,17},{17,33},{33,49},{49,1},{2,18}... | collective-permute-start | bytes 1966088 | tf_op jit(solution)/shard_map/ppermute | solution.py:19
  361.3 8.7 %collective-permute-start.39 = (bf16[32,1408]{1,0:T(8,128)(2,1)S(1)}, bf16[32,1408]{1,0:T(8,128)(2,1)S(1)}, u32[]{:S(2)}, u32[]{:S(2)}) collective-permute-start(bf16[32,1408]{1,0:T(8,128)(2,1)S(1)} %get-tuple-element.128), channel_id=1, source_target_pairs={{0,12},{4,0},{8,4},{12,8},{1,13},{5,1},{9,5},{13,9},{2,14},{6,2},{... | collective-permute-start | bytes 270344 | tf_op jit(solution)/shard_map/ppermute | solution.py:19
  370.7 14.1 %collective-permute-start.58 = (bf16[256,704]{0,1:T(8,128)(2,1)S(1)}, bf16[256,704]{0,1:T(8,128)(2,1)S(1)}, u32[]{:S(2)}, u32[]{:S(2)}) collective-permute-start(bf16[256,704]{0,1:T(8,128)(2,1)S(1)} %copy-done.40), channel_id=1, source_target_pairs={{0,48},{16,0},{32,16},{48,32},{1,49},{17,1},{33,17},{49,33},{2,50}... | collective-permute-start | bytes 1081352 | tf_op jit(solution)/shard_map/ppermute | solution.py:19
  384.2 11.0 %collective-permute-start.53 = (bf16[256,704]{0,1:T(8,128)(2,1)S(1)}, bf16[256,704]{0,1:T(8,128)(2,1)S(1)}, u32[]{:S(2)}, u32[]{:S(2)}) collective-permute-start(bf16[256,704]{0,1:T(8,128)(2,1)S(1)} %copy-done.39), channel_id=1, source_target_pairs={{0,2},{2,0},{1,3},{3,1},{4,6},{6,4},{5,7},{7,5},{8,10},{10,8},{9,1... | collective-permute-start | bytes 1081352 | tf_op jit(solution)/shard_map/ppermute | solution.py:19
  384.3 8.4 %collective-permute-start.57 = (bf16[256,704]{0,1:T(8,128)(2,1)}, bf16[256,704]{0,1:T(8,128)(2,1)S(1)}, u32[]{:S(2)}, u32[]{:S(2)}) collective-permute-start(bf16[256,704]{0,1:T(8,128)(2,1)} %collective-permute-done.56), channel_id=1, source_target_pairs={{0,2},{2,0},{1,3},{3,1},{4,6},{6,4},{5,7},{7,5},{8,10},{10,8},{9,1... | collective-permute-start | bytes 1081352 | tf_op jit(solution)/shard_map/ppermute | solution.py:19
  384.8 11.5 %collective-permute-start.55 = (bf16[256,704]{0,1:T(8,128)(2,1)S(1)}, bf16[256,704]{0,1:T(8,128)(2,1)S(1)}, u32[]{:S(2)}, u32[]{:S(2)}) collective-permute-start(bf16[256,704]{0,1:T(8,128)(2,1)S(1)} %collective-permute-done.54), channel_id=1, source_target_pairs={{0,2},{2,0},{1,3},{3,1},{4,6},{6,4},{5,7},{7,5},{8,10},{10,8},{9,1... | collective-permute-start | bytes 1081352 | tf_op jit(solution)/shard_map/ppermute | solution.py:19
  385.3 11.9 %collective-permute-start.59 = (bf16[256,704]{0,1:T(8,128)(2,1)S(1)}, bf16[256,704]{0,1:T(8,128)(2,1)S(1)}, u32[]{:S(2)}, u32[]{:S(2)}) collective-permute-start(bf16[256,704]{0,1:T(8,128)(2,1)S(1)} %collective-permute-done.58), channel_id=1, source_target_pairs={{0,2},{2,0},{1,3},{3,1},{4,6},{6,4},{5,7},{7,5},{8,10},{10,8},{9,1... | collective-permute-start | bytes 1081352 | tf_op jit(solution)/shard_map/ppermute | solution.py:19
  408.5 12.3 %collective-permute-start.62 = (bf16[128,704]{1,0:T(8,128)(2,1)}, bf16[128,704]{1,0:T(8,128)(2,1)}, u32[]{:S(2)}, u32[]{:S(2)}) collective-permute-start(bf16[128,704]{1,0:T(8,128)(2,1)} %get-tuple-element.120), channel_id=1, source_target_pairs={{0,12},{4,0},{8,4},{12,8},{1,13},{5,1},{9,5},{13,9},{2,14},{6,2},{... | collective-permute-start | bytes 540680 | tf_op jit(solution)/shard_map/ppermute | solution.py:19
  422.5 10.1 %collective-permute-start.63 = (bf16[256,704]{1,0:T(8,128)(2,1)}, bf16[256,704]{1,0:T(8,128)(2,1)S(1)}, u32[]{:S(2)}, u32[]{:S(2)}) collective-permute-start(bf16[256,704]{1,0:T(8,128)(2,1)} %pad_maximum_fusion.14), channel_id=1, source_target_pairs={{0,12},{4,0},{8,4},{12,8},{1,13},{5,1},{9,5},{13,9},{2,14},{6,2},{... | collective-permute-start | bytes 1081352 | tf_op jit(solution)/shard_map/ppermute | solution.py:19
  426.9 10.8 %collective-permute-start.61 = (bf16[256,704]{1,0:T(8,128)(2,1)S(1)}, bf16[256,704]{1,0:T(8,128)(2,1)S(1)}, u32[]{:S(2)}, u32[]{:S(2)}) collective-permute-start(bf16[256,704]{1,0:T(8,128)(2,1)S(1)} %pad_maximum_fusion.13), channel_id=1, source_target_pairs={{0,4},{4,8},{8,12},{12,0},{1,5},{5,9},{9,13},{13,1},{2,6},{6,10},{... | collective-permute-start | bytes 1081352 | tf_op jit(solution)/shard_map/ppermute | solution.py:19
  428.6 10.5 %collective-permute-start.40 = (f32[2,32]{1,0:T(2,128)S(1)}, f32[2,32]{1,0:T(2,128)S(1)}, u32[]{:S(2)}, u32[]{:S(2)}) collective-permute-start(f32[2,32]{1,0:T(2,128)S(1)} %pad_maximum_fusion.24), channel_id=1, source_target_pairs={{0,1},{1,0},{2,3},{3,2},{4,5},{5,4},{6,7},{7,6},{8,9},{9,8},{10,11... | collective-permute-start | bytes 776 | tf_op jit(solution)/shard_map/ppermute | solution.py:19
  (98 other events, 673.4 us)
Sparse Core Ops, SparseCore 0:
  62.2 46.3 all-gather.2
